TPU v7x, 512 devices: a whole 4x4x16 slice. The times are simulated.
512 devices in a mesh: sub: 8 (over y, z_hi), row: 8 (over z_lo), col: 8 (over x, core).
Axes of the slice: x: 4, y: 4, z: 16 (z_hi: 2, z_lo: 8; z = z_hi * 8 + z_lo), core: 2. Of those that a mesh axis runs over, the one named last changes fastest.
Arguments:
- root_inverse: float32 [8192, 8192], P(('sub', 'row'), 'col')
- panel: float32 [8192, 2048], P(('sub', 'row'), 'col'), may hold values from -0.125 to 0.125
- pattern: int32 [64, 16], P(('sub', 'row'), 'col'), may hold values from 0 to 1, as said below
- diag_inverse: float32 [2048, 2048], P(('sub', 'row'), 'col')
Outputs:
- off_block: float32 [8192, 2048], P(('sub', 'row'), 'col')
- diag_block: float32 [2048, 2048], P(('sub', 'row'), 'col')
Inputs may be any that keep to these rules, and one draw needn't show every extreme that they name: `pattern`: in every tile row, each aligned group of 2 tile columns (those of one index of col) has exactly one tile marked 1.
All inputs are finite; a program needn't handle non-finite values.
Results may differ from a plain program's by a relative error of at most 0.000078.
Values sent between devices are 32-bit elements; how exact they have to be, the bound alone decides.
A program may use at most 64 MiB of HBM per device.

v0:
```python
import jax
import jax.numpy as jnp
from jax import lax
from jax.sharding import PartitionSpec as P

highest = lax.Precision.HIGHEST


def rows_of_inverse(root_inverse):
    return lax.all_gather(root_inverse, "col", axis=1, tiled=True)


def local(root_inverse, panel, pattern, diag_inverse):
    tile_rows = panel.shape[0]
    marked = pattern[0].astype(jnp.float32)
    column_mask = jnp.repeat(marked, tile_rows)
    masked_panel = panel * column_mask[None, :]
    inverse_full = rows_of_inverse(root_inverse)
    accumulated = jnp.dot(
        inverse_full,
        lax.all_gather(masked_panel, ("sub", "row"), axis=0, tiled=True),
        precision=highest,
        preferred_element_type=jnp.float32,
    )
    off_block = -(accumulated * column_mask[None, :])
    panel_full_row = lax.all_gather(masked_panel, "col", axis=1, tiled=True)
    contribution = lax.dot_general(
        panel_full_row,
        off_block,
        (((0,), (0,)), ((), ())),
        precision=highest,
        preferred_element_type=jnp.float32,
    )
    update = lax.psum_scatter(contribution, ("sub", "row"), scatter_dimension=0, tiled=True)
    diag_block = diag_inverse - update
    return (off_block, diag_block)


def solution(mesh):
    in_specs = (
        P(("sub", "row"), "col"),
        P(("sub", "row"), "col"),
        P(("sub", "row"), "col"),
        P(("sub", "row"), "col"),
    )
    out_specs = (P(("sub", "row"), "col"), P(("sub", "row"), "col"))
    return jax.shard_map(local, mesh=mesh, in_specs=in_specs, out_specs=out_specs, check_vma=False)
```

profile of v0, /device:TPU:2, one launch (start us, length us, event | category | flops | bytes accessed | tf_op | source)
XLA Modules:
  0.0 950.3 jit_solution(14879854118065150119)
XLA Ops:
  7.2 0.0 all-gather.6.cloned.1.call-start
  7.2 0.7 all-gather.6.cloned.1.call-update
  7.9 0.0 all-gather.4.cloned.1.call-start
  7.9 0.7 convert_bitcast_fusion
  8.6 0.1 broadcast_bitcast_fusion
  8.7 1.6 broadcast_multiply_fusion
  10.2 0.0 all-gather.4.cloned.1.call-update
  10.3 0.0 all-gather.8.cloned.1.call-start
  10.3 0.7 all-gather.8.cloned.1.call-update
  11.0 0.0 reduce-scatter.2.cloned.1.call-start
  11.1 42.3 %all-gather.6.cloned.1.call-done = f32[128,8192]{1,0:T(8,128)} async-done(((f32[128,1024]{1,0:T(8,128)}), f32[128,8192]{1,0:T(8,128)}) %all-gather.6.cloned.1.call-update) | async-done | bytes 4194320 | tf_op jit(solution)/shard_map/all_gather | solution.py:10
  53.4 161.6 %all-gather.4.cloned.1.call-done = f32[8192,256]{1,0:T(8,128)} async-done(((f32[128,256]{1,0:T(8,128)}), f32[8192,256]{1,0:T(8,128)}) %all-gather.4.cloned.1.call-update) | async-done | bytes 8388624 | tf_op jit(solution)/shard_map/all_gather | solution.py:21
  215.0 16.3 %fusion = f32[256,128]{1,0:T(8,128)S(1)} fusion(f32[8192,256]{1,0:T(8,128)} %all-gather.4.cloned.1.call-done, f32[128,8192]{1,0:T(8,128)} %all-gather.6.cloned.1.call-done, f32[256]{0:T(256)S(1)} %broadcast_bitcast_fusion), kind=kOutput, calls=%fused_computation.1 | convolution fusion | flops 3221291008 | bytes 12715008 | tf_op jit(solution)/shard_map/dot_general | solution.py:19
  231.3 0.0 copy-start
  231.3 11.0 %all-gather.8.cloned.1.call-done = f32[128,2048]{1,0:T(8,128)} async-done(((f32[128,256]{1,0:T(8,128)}), f32[128,2048]{1,0:T(8,128)}) %all-gather.8.cloned.1.call-update) | async-done | bytes 1048592 | tf_op jit(solution)/shard_map/all_gather | solution.py:26
  242.3 4.4 fusion.1
  246.7 0.0 reduce-scatter.2.cloned.1.call-update
  246.7 0.8 copy.6
  247.5 694.9 %reduce-scatter.2.cloned.1.call-done = f32[32,256]{1,0:T(8,128)} async-done(((f32[2048,256]{1,0:T(8,128)}), f32[32,256]{1,0:T(8,128)}) %reduce-scatter.2.cloned.1.call-update) | async-done | bytes 32784 | tf_op jit(solution)/shard_map/reduce_scatter | solution.py:34
  942.4 0.0 copy-done
  942.4 1.4 sub.3
Async XLA Ops:
  7.2 46.2 %all-gather.6.cloned.1.call-start = ((), (), s32[]{:S(2)}) async-start(), calls=%async_computation.2 | async-start | bytes 4718592 | tf_op jit(solution)/shard_map/all_gather | solution.py:10
  7.9 207.1 %all-gather.4.cloned.1.call-start = ((), (), s32[]{:S(2)}) async-start(), calls=%async_computation.1 | async-start | bytes 8519680 | tf_op jit(solution)/shard_map/all_gather | solution.py:21
  10.3 232.0 %all-gather.8.cloned.1.call-start = ((), (), s32[]{:S(2)}) async-start(), calls=%async_computation.3 | async-start | bytes 1179648 | tf_op jit(solution)/shard_map/all_gather | solution.py:26
  11.0 931.4 %reduce-scatter.2.cloned.1.call-start = ((), (), s32[]{:S(2)}) async-start(), calls=%async_computation.4 | async-start | bytes 2129920 | tf_op jit(solution)/shard_map/reduce_scatter | solution.py:34
  231.3 711.1 %copy-start = (f32[32,256]{1,0:T(8,128)S(1)}, f32[32,256]{1,0:T(8,128)}, u32[]{:S(2)}) copy-start(f32[32,256]{1,0:T(8,128)} %param.7) | copy-start | bytes 98308
Sparse Core Ops, SparseCore 0:
  10.1 43.1 all-gather.5
  56.9 158.0 all-gather.3
  217.7 24.5 all-gather.7
  246.8 695.4 reduce-scatter.1
where the time goes:
time: 951 us; the launch traced here: 950 us
  waiting for transfers between devices  911 us (96%)
  matrix products  20.7 us (2%)
  between operations  13.8 us (1%)
    reduce_scatter x1, waiting for transfers between devices, local(): lax.psum_scatter(contribution, ('sub', 'row'), scatter_dimension=0, tiled...  695 us
    all_gather x1, waiting for transfers between devices, local(): lax.all_gather(masked_panel, ('sub', 'row'), axis=0, tiled=True)  162 us
    all_gather x1, waiting for transfers between devices, rows_of_inverse(): return lax.all_gather(root_inverse, 'col', axis=1, tiled=True)  42.3 us
  transfers between devices with their start and end apart: 4, of which 4 were waited for; matrix products, arithmetic and copies ran while one was open for 2% of the time, Pallas kernels for 0%

commit v1 on v0

--- a/solution.py
+++ b/solution.py
@@ -7,7 +7,9 @@
 
 
 def rows_of_inverse(root_inverse):
-    return lax.all_gather(root_inverse, "col", axis=1, tiled=True)
+    return jnp.concatenate(
+        lax.all_to_all(jnp.stack([root_inverse] * lax.axis_size("col")), "col", 0, 0), axis=1
+    )
 
 
 def local(root_inverse, panel, pattern, diag_inverse):

time: 951 us -> 909 us (0.956)
  the two profiles are of different devices: /device:TPU:2 before, /device:TPU:4 now
where the time goes in v1:
time: 909 us; the launch traced here: 908 us
  waiting for transfers between devices  856 us (94%)
  matrix products  20.7 us (2%)
  between operations  13.8 us (2%)
  starting transfers between devices  10.5 us (1%)
    reduce_scatter x1, waiting for transfers between devices, local(): lax.psum_scatter(contribution, ('sub', 'row'), scatter_dimension=0, tiled...  695 us
    all_gather x1, waiting for transfers between devices, local(): lax.all_gather(masked_panel, ('sub', 'row'), axis=0, tiled=True)  103 us
    all_to_all x1, waiting for transfers between devices, rows_of_inverse(): lax.all_to_all(jnp.stack([root_inverse] * lax.axis_size('col')), 'col', 0...  45.8 us
  transfers between devices with their start and end apart: 4, of which 4 were waited for; matrix products, arithmetic and copies ran while one was open for 2% of the time, Pallas kernels for 0%

profile of v1, /device:TPU:4, one launch (start us, length us, event | category | flops | bytes accessed | tf_op | source)
XLA Modules:
  0.0 908.3 jit_solution(3263827340082395031)
XLA Ops:
  7.2 0.0 all-gather.3.cloned.1.call-start
  7.2 0.7 convert_bitcast_fusion
  7.9 0.1 broadcast_bitcast_fusion
  7.9 1.6 broadcast_multiply_fusion
  9.5 0.0 all-gather.3.cloned.1.call-update
  9.5 1.2 copy.7
  10.8 2.2 stack.2
  13.0 10.4 %all-to-all-start = ((f32[8,128,1024]{1,2,0:T(8,128)}), f32[8,128,1024]{1,2,0:T(8,128)}, u32[]{:S(2)}, u32[]{:S(2)}) async-start(f32[8,128,1024]{1,2,0:T(8,128)} %stack.2), calls=%async_computation | async-start | bytes 8388608 | tf_op jit(solution)/shard_map/all_to_all | solution.py:11
  23.4 0.0 all-gather.5.cloned.1.call-start
  23.4 0.7 all-gather.5.cloned.1.call-update
  24.1 0.0 reduce-scatter.2.cloned.1.call-start
  24.1 45.8 %all-to-all-done = f32[8,128,1024]{1,2,0:T(8,128)} async-done(((f32[8,128,1024]{1,2,0:T(8,128)}), f32[8,128,1024]{1,2,0:T(8,128)}, u32[]{:S(2)}, u32[]{:S(2)}) %all-to-all-start) | async-done | bytes 4194336 | tf_op jit(solution)/shard_map/all_to_all | solution.py:11
  69.9 102.9 %all-gather.3.cloned.1.call-done = f32[8192,256]{1,0:T(8,128)} async-done(((f32[128,256]{1,0:T(8,128)}), f32[8192,256]{1,0:T(8,128)}) %all-gather.3.cloned.1.call-update) | async-done | bytes 8388624 | tf_op jit(solution)/shard_map/all_gather | solution.py:23
  172.9 16.3 %fusion = f32[256,128]{1,0:T(8,128)S(1)} fusion(f32[8192,256]{1,0:T(8,128)} %all-gather.3.cloned.1.call-done, f32[128,8192]{0,1:T(8,128)} %bitcast.3, f32[256]{0:T(256)S(1)} %broadcast_bitcast_fusion), kind=kOutput, calls=%fused_computation.1 | convolution fusion | flops 3221291008 | bytes 12715008 | tf_op jit(solution)/shard_map/dot_general | solution.py:21
  189.2 0.0 copy-start
  189.2 11.3 %all-gather.5.cloned.1.call-done = f32[128,2048]{1,0:T(8,128)} async-done(((f32[128,256]{1,0:T(8,128)}), f32[128,2048]{1,0:T(8,128)}) %all-gather.5.cloned.1.call-update) | async-done | bytes 1048592 | tf_op jit(solution)/shard_map/all_gather | solution.py:28
  200.5 4.4 fusion.1
  204.9 0.0 reduce-scatter.2.cloned.1.call-update
  204.9 0.8 copy.8
  205.7 694.7 %reduce-scatter.2.cloned.1.call-done = f32[32,256]{1,0:T(8,128)} async-done(((f32[2048,256]{1,0:T(8,128)}), f32[32,256]{1,0:T(8,128)}) %reduce-scatter.2.cloned.1.call-update) | async-done | bytes 32784 | tf_op jit(solution)/shard_map/reduce_scatter | solution.py:36
  900.4 0.0 copy-done
  900.4 1.4 sub.3
Async XLA Ops:
  7.2 165.7 %all-gather.3.cloned.1.call-start = ((), (), s32[]{:S(2)}) async-start(), calls=%async_computation.2 | async-start | bytes 8519680 | tf_op jit(solution)/shard_map/all_gather | solution.py:23
  13.0 57.0 %all-to-all-start = ((f32[8,128,1024]{1,2,0:T(8,128)}), f32[8,128,1024]{1,2,0:T(8,128)}, u32[]{:S(2)}, u32[]{:S(2)}) async-start(f32[8,128,1024]{1,2,0:T(8,128)} %stack.2), calls=%async_computation | async-start | bytes 8388608 | tf_op jit(solution)/shard_map/all_to_all | solution.py:11
  23.4 177.1 %all-gather.5.cloned.1.call-start = ((), (), s32[]{:S(2)}) async-start(), calls=%async_computation.3 | async-start | bytes 1179648 | tf_op jit(solution)/shard_map/all_gather | solution.py:28
  24.1 876.3 %reduce-scatter.2.cloned.1.call-start = ((), (), s32[]{:S(2)}) async-start(), calls=%async_computation.4 | async-start | bytes 2129920 | tf_op jit(solution)/shard_map/reduce_scatter | solution.py:36
  189.2 711.2 %copy-start = (f32[32,256]{1,0:T(8,128)S(1)}, f32[32,256]{1,0:T(8,128)}, u32[]{:S(2)}) copy-start(f32[32,256]{1,0:T(8,128)} %param.7) | copy-start | bytes 98308
Sparse Core Ops, SparseCore 0:
  11.5 161.3 all-gather.2
  175.6 24.8 all-gather.4
  205.0 695.3 reduce-scatter.1
